TPU v7x, 256 devices: a whole 4x4x8 slice. The times are simulated.
256 devices in a mesh: dp: 8 (over z_lo, core), seq: 32 (over y, x, z_hi).
Axes of the slice: x: 4, y: 4, z: 8 (z_hi: 2, z_lo: 4; z = z_hi * 4 + z_lo), core: 2. Of those that a mesh axis runs over, the one named last changes fastest.
Arguments:
- queries: bfloat16 [16, 2048, 4096], P('dp', 'seq'), may hold values from -40 to 40
- keys: bfloat16 [16, 2048, 4096], P('dp', 'seq'), may hold values from -40 to 40
- values: bfloat16 [16, 2048, 4096], P('dp', 'seq'), may hold values from -6 to 6
- out_grad: bfloat16 [16, 2048, 4096], P('dp', 'seq'), may hold values from -4400 to 4400
- q_gain: float32 [32, 128], replicated, may hold values from 0.5 to 6
- k_gain: float32 [32, 128], replicated, may hold values from 0.5 to 6
Outputs:
- q_grad: bfloat16 [16, 2048, 4096], P('dp', 'seq')
- k_grad: bfloat16 [16, 2048, 4096], P('dp', 'seq')
- v_grad: bfloat16 [16, 2048, 4096], P('dp', 'seq')
- q_gain_grad: float32 [32, 128], P('seq')
- k_gain_grad: float32 [32, 128], P('seq')
All inputs are finite; a program needn't handle non-finite values.
Results may differ from a plain program's by a relative error of at most 0.004.
The roundings to bfloat16 on the way count: a program that leaves them out, or rounds other values in their place, can miss the bound.
Values may be sent and summed in bfloat16 or wider, within the bound.
A program may use at most 64 MiB of HBM per device.

v0:
```python
import math

import jax
import jax.numpy as jnp
from jax import lax
from jax.sharding import PartitionSpec as P


def normalize(raw, gain):
    widened = raw.astype(jnp.float32)
    rate = lax.rsqrt(jnp.mean(widened * widened, axis=-1, keepdims=True) + 1e-06)
    unit = widened * rate
    return (unit, rate, (unit * gain).astype(jnp.bfloat16))


def norm_back(unit, rate, grad, gain):
    grad_wide = lax.optimization_barrier(grad).astype(jnp.float32)
    scaled = gain * grad_wide
    inner = jnp.mean(scaled * unit, axis=-1, keepdims=True)
    result = (rate * (scaled - unit * inner)).astype(jnp.bfloat16)
    term = jnp.sum(grad_wide * unit, axis=tuple(range(unit.ndim - 2)))
    return (result, term)


def attend(query_normed, key_normed, value_rows, grad_rows):
    length, local, depth = query_normed.shape
    rows = min(512, length)
    blocks = length // rows
    scale = depth ** (-0.5)
    query_blocks = query_normed.reshape(blocks, rows, local, depth)
    grad_blocks = grad_rows.reshape(blocks, rows, local, depth)

    def advance(carry, block):
        key_acc, value_acc = carry
        query_part, grad_part = block
        scores = (
            jnp.einsum("qhd,khd->hqk", query_part, key_normed, preferred_element_type=jnp.float32)
            * scale
        )
        scores = scores - jnp.max(scores, axis=-1, keepdims=True)
        weights = jnp.exp(scores)
        probs = weights / jnp.sum(weights, axis=-1, keepdims=True)
        probs_low = probs.astype(jnp.bfloat16)
        prob_grad = jnp.einsum(
            "qhd,khd->hqk", grad_part, value_rows, preferred_element_type=jnp.float32
        )
        row_dot = jnp.sum(probs * prob_grad, axis=-1, keepdims=True)
        score_grad = (probs * (prob_grad - row_dot) * scale).astype(jnp.bfloat16)
        value_acc = value_acc + jnp.einsum(
            "hqk,qhd->khd", probs_low, grad_part, preferred_element_type=jnp.float32
        )
        key_acc = key_acc + jnp.einsum(
            "hqk,qhd->khd", score_grad, query_part, preferred_element_type=jnp.float32
        )
        query_grad = jnp.einsum(
            "hqk,khd->qhd", score_grad, key_normed, preferred_element_type=jnp.float32
        )
        return ((key_acc, value_acc), query_grad.astype(jnp.bfloat16))

    zeros = jnp.zeros((length, local, depth), jnp.float32)
    (key_acc, value_acc), query_grads = lax.scan(
        advance, (zeros, zeros), (query_blocks, grad_blocks)
    )
    return (
        query_grads.reshape(length, local, depth),
        key_acc.astype(jnp.bfloat16),
        value_acc.astype(jnp.bfloat16),
    )


def body(queries, keys, values, out_grad, q_gain, k_gain):
    seq_count = lax.axis_size("seq")
    sample_count, tok_rows, width = queries.shape
    heads, depth = q_gain.shape
    local = heads // seq_count
    length = tok_rows * seq_count
    factor = 1.0 / math.sqrt(sample_count * lax.axis_size("dp") * length)
    token_shape = (sample_count, tok_rows, heads, depth)
    head_shape = (length, local, depth)
    q_unit, q_rate, q_normed = normalize(queries.reshape(token_shape), q_gain)
    k_unit, k_rate, k_normed = normalize(keys.reshape(token_shape), k_gain)
    q_sent = q_normed.reshape(sample_count, tok_rows, width)
    k_sent = k_normed.reshape(sample_count, tok_rows, width)

    def per_item(group):
        query_rows, key_rows, value_rows, grad_rows = group
        query_grad, key_grad, value_grad = attend(
            query_rows.reshape(head_shape),
            key_rows.reshape(head_shape),
            value_rows.reshape(head_shape),
            grad_rows.reshape(head_shape),
        )
        return (
            query_grad.reshape(length, local * depth),
            key_grad.reshape(length, local * depth),
            value_grad.reshape(length, local * depth),
        )

    computed = lax.map(
        per_item,
        (
            lax.all_to_all(q_sent, "seq", split_axis=2, concat_axis=1, tiled=True),
            lax.all_to_all(k_sent, "seq", split_axis=2, concat_axis=1, tiled=True),
            lax.all_to_all(values, "seq", split_axis=2, concat_axis=1, tiled=True),
            lax.all_to_all(out_grad, "seq", split_axis=2, concat_axis=1, tiled=True),
        ),
    )
    results = (
        lax.all_to_all(computed[0], "seq", split_axis=1, concat_axis=2, tiled=True),
        lax.all_to_all(computed[1], "seq", split_axis=1, concat_axis=2, tiled=True),
        lax.all_to_all(computed[2], "seq", split_axis=1, concat_axis=2, tiled=True),
    ) + tuple(computed[3:])
    q_back, q_term = norm_back(q_unit, q_rate, results[0].reshape(token_shape), q_gain)
    k_back, k_term = norm_back(k_unit, k_rate, results[1].reshape(token_shape), k_gain)
    q_grad = q_back.reshape(sample_count, tok_rows, width)
    k_grad = k_back.reshape(sample_count, tok_rows, width)
    shares = (
        lax.psum_scatter(q_term, "seq", scatter_dimension=0, tiled=True),
        lax.psum_scatter(k_term, "seq", scatter_dimension=0, tiled=True),
    )
    totals = lax.psum((shares[0], shares[1]), "dp")
    return (q_grad, k_grad, results[2], totals[0] * factor, totals[1] * factor)


def solution(mesh):
    return jax.shard_map(
        body,
        mesh=mesh,
        in_specs=(
            P("dp", "seq", None),
            P("dp", "seq", None),
            P("dp", "seq", None),
            P("dp", "seq", None),
            P(),
            P(),
        ),
        out_specs=(
            P("dp", "seq", None),
            P("dp", "seq", None),
            P("dp", "seq", None),
            P("seq", None),
            P("seq", None),
        ),
        check_vma=False,
    )
```

profile of v0, /device:TPU:32, one launch (start us, length us, event | category | flops | bytes accessed | tf_op | source)
XLA Modules:
  0.0 656.9 jit_solution(2395627948682681512)
XLA Ops:
  0.6 5.0 copy.119
  5.7 2.7 multiply_reduce_fusion.2
  9.1 12.1 %fusion.32 = bf16[2,64,4096]{1,0,2:T(2,128)(2,1)} fusion(f32[4096]{0:T(1024)S(1)} %bitcast.198, f32[2,64,32]{1,0,2:T(2,128)S(1)} %copy.121, bf16[2,64,4096]{1,0,2:T(2,128)(2,1)S(1)} %copy.119), kind=kLoop, calls=%fused_computation.48 | loop fusion | flops 2097152 | bytes 2129920 | tf_op jit(solution)/shard_map/convert_element_type | solution.py:13
  21.2 5.8 reshape.147
  27.0 13.0 %all-to-all-start = ((bf16[32,2,8192]{2,1,0:T(2,128)(2,1)}), bf16[32,2,8192]{2,1,0:T(2,128)(2,1)S(1)}, u32[]{:S(2)}, u32[]{:S(2)}) async-start(bf16[32,2,8192]{2,1,0:T(2,128)(2,1)} %reshape.147), calls=%async_computation | async-start | bytes 2097152 | tf_op jit(solution)/shard_map/all_to_all | solution.py:102
  48.0 2.5 multiply_convert_fusion.1
  50.5 5.0 copy.127
  55.5 2.2 reshape.151
  57.8 15.2 %all-to-all-done = bf16[32,2,8192]{2,1,0:T(2,128)(2,1)S(1)} async-done(((bf16[32,2,8192]{2,1,0:T(2,128)(2,1)}), bf16[32,2,8192]{2,1,0:T(2,128)(2,1)S(1)}, u32[]{:S(2)}, u32[]{:S(2)}) %all-to-all-start) | async-done | bytes 1048608 | tf_op jit(solution)/shard_map/all_to_all | solution.py:102
  73.0 4.7 all-to-all-start.2
  77.7 5.0 copy.123
  85.0 18.6 %all-to-all-done.2 = bf16[32,2,8192]{2,1,0:T(2,128)(2,1)} async-done(((bf16[32,2,8192]{2,1,0:T(2,128)(2,1)}), bf16[32,2,8192]{2,1,0:T(2,128)(2,1)}, u32[]{:S(2)}, u32[]{:S(2)}) %all-to-all-start.2) | async-done | bytes 1048608 | tf_op jit(solution)/shard_map/all_to_all | solution.py:103
  103.6 4.9 all-to-all-start.1
  108.5 5.0 copy.129
  113.5 2.2 reshape.153
  115.8 17.0 %all-to-all-done.1 = bf16[32,2,8192]{2,1,0:T(2,128)(2,1)} async-done(((bf16[32,2,8192]{2,1,0:T(2,128)(2,1)}), bf16[32,2,8192]{2,1,0:T(2,128)(2,1)}, u32[]{:S(2)}, u32[]{:S(2)}) %all-to-all-start.1) | async-done | bytes 1048608 | tf_op jit(solution)/shard_map/all_to_all | solution.py:105
  132.8 4.7 all-to-all-start.3
  138.9 3.8 copy.122
  142.7 5.0 reshape.152
  147.7 3.8 copy.128
  151.5 5.0 reshape.150
  156.6 3.9 copy.124
  162.0 5.0 reshape.154
  167.0 3.8 copy.130
  170.8 121.1 %while.30 = (s32[]{:T(128)}, bf16[2,2048,128]{2,1,0:T(8,128)(2,1)}, bf16[2,2048,128]{1,2,0:T(8,128)(2,1)}, bf16[2,2048,128]{1,2,0:T(8,128)(2,1)}, bf16[2,2048,12...) while((s32[]{:T(128)}, bf16[2,2048,128]{2,1,0:T(8,128)(2,1)}, ...), condition=%wide.region_8.9_spmd, body=%wide.region_2.8_spmd.sunk | while | flops 1365834240 | bytes 86139816 | solution.py:99
  176.8 51.6 %while.31 = (s32[]{:T(128)}, f32[2048,1,128]{0,2,1:T(8,128)S(1)}, f32[2048,1,128]{0,2,1:T(8,128)S(1)}, bf16[4,512,1,128]{3,1,2,0:T(8,128)(2,1)}, bf16[4,512,1,12...) while((s32[]{:T(128)}, f32[2048,1,128]{0,2,1:T(8,128)S(1)}, ...), condition=%wide.region_7.7_spmd.clone, body=%wide.region_3.6_spmd.clone.sunk | while | flops 1365309952 | bytes 77749960 | solution.py:61
  180.4 3.6 fusion.62
  193.3 3.6 fusion.62
  206.2 3.6 fusion.62
  219.1 3.6 fusion.62
  237.4 51.6 %while.31 = (s32[]{:T(128)}, f32[2048,1,128]{0,2,1:T(8,128)S(1)}, f32[2048,1,128]{0,2,1:T(8,128)S(1)}, bf16[4,512,1,128]{3,1,2,0:T(8,128)(2,1)}, bf16[4,512,1,12...) while((s32[]{:T(128)}, f32[2048,1,128]{0,2,1:T(8,128)S(1)}, ...), condition=%wide.region_7.7_spmd.clone, body=%wide.region_3.6_spmd.clone.sunk | while | flops 1365309952 | bytes 77749960 | solution.py:61
  240.9 3.6 fusion.62
  253.8 3.6 fusion.62
  266.7 3.6 fusion.62
  279.6 3.6 fusion.62
  291.9 3.7 copy.133
  295.6 10.6 %all-to-all-start.4 = ((bf16[2,2048,128]{2,0,1:T(2,128)(2,1)}), bf16[2,2048,128]{2,0,1:T(2,128)(2,1)S(1)}, u32[]{:S(2)}, u32[]{:S(2)}) async-start(bf16[2,2048,128]{2,0,1:T(2,128)(2,1)} %copy.133), calls=%async_computation.4 | async-start | bytes 2097152 | tf_op jit(solution)/shard_map/all_to_all | solution.py:109
  308.2 28.3 %all-to-all-done.4 = bf16[2,2048,128]{2,0,1:T(2,128)(2,1)S(1)} async-done(((bf16[2,2048,128]{2,0,1:T(2,128)(2,1)}), bf16[2,2048,128]{2,0,1:T(2,128)(2,1)S(1)}, u32[]{:S(2)}, u32[]{:S(2)}) %all-to-all-start.4) | async-done | bytes 1048608 | tf_op jit(solution)/shard_map/all_to_all | solution.py:109
  336.5 4.7 all-to-all-start.5
  341.8 3.7 copy.143
  345.5 3.8 copy.134
  349.3 34.3 %fusion.30 = (f32[32,128]{1,0:T(8,128)S(1)}, f32[2,64,32]{1,0,2:T(2,128)S(1)}) fusion(bf16[2,64,32,128]{1,0,3,2:T(2,128)(2,1)} %bitcast.180, f32[2,64,32]{1,0,2:T(2,128)S(1)} %copy-done.11, bf16[2,64,4096]{1,0,2:T(2,128)(2,1)S(1)} %copy-done.3, f32[32,128]{1,0:T(8,128)S(1)} %copy-done.13, bf16[2,64,32,128]{1,0,3,2:T(2,128)(2,1)S(1)} %bitcast.176), kind=kLoop, calls=%fused_computation.45 | loop fusion | flops 5234688 | bytes 3211264 | tf_op jit(solution)/shard_map/reduce_sum | solution.py:21
  383.6 12.5 %all-to-all-start.6 = ((bf16[2,2048,128]{2,0,1:T(2,128)(2,1)}), bf16[2,2048,128]{2,0,1:T(2,128)(2,1)}, u32[]{:S(2)}, u32[]{:S(2)}) async-start(bf16[2,2048,128]{2,0,1:T(2,128)(2,1)} %copy.143), calls=%async_computation.6 | async-start | bytes 2097152 | tf_op jit(solution)/shard_map/all_to_all | solution.py:111
  396.1 8.0 %fusion.29 = bf16[2,64,32,128]{1,0,3,2:T(2,128)(2,1)} fusion(bf16[2,64,32,128]{1,0,3,2:T(2,128)(2,1)} %bitcast.181, f32[2,64,32]{1,0,2:T(2,128)S(1)} %copy.136, f32[32,128]{1,0:T(8,128)S(1)} %copy-done.13, f32[2,64,32]{1,0,2:T(2,128)S(1)} %copy-done.11, bf16[2,64,4096]{1,0,2:T(2,128)(2,1)S(1)} %copy-done.3), kind=kLoop, calls=%fused_computation.44 | loop fusion | flops 4194304 | bytes 3194880 | tf_op jit(solution)/shard_map/convert_element_type | solution.py:20
  406.2 5.4 copy.146
  415.3 2.3 reshape.138
  417.6 224.9 %all-reduce.2 = (f32[32,128]{1,0:T(8,128)S(1)}, f32[32,128]{1,0:T(8,128)S(1)}) all-reduce(f32[32,128]{1,0:T(8,128)S(1)} %get-tuple-element.229, f32[32,128]{1,0:T(8,128)S(1)} %get-tuple-element.227), channel_id=2, replica_groups=mesh['dp'=8,'seq'=32] {'seq'}, use_global_device_ids=true, to_apply=%region_12.13.clone | all-reduce | flops 8192 | bytes 65536
  643.2 10.0 %all-reduce.3 = (f32[1,128]{1,0:T(1,128)S(1)}, f32[1,128]{1,0:T(1,128)S(1)}) all-reduce(f32[1,128]{1,0:T(1,128)S(1)} %get-tuple-element.274, f32[1,128]{1,0:T(1,128)S(1)} %get-tuple-element.273), channel_id=1, replica_groups=mesh['dp'=8,'seq'=32] {'dp'}, use_global_device_ids=true, to_apply=%region_13.14 | all-reduce | flops 256 | bytes 2048 | tf_op jit(solution)/shard_map/psum | solution.py:121
  (174 shorter events, 117.8 us)
Async XLA Ops:
  0.6 8.5 %copy-start.12 = (f32[32,128]{1,0:T(8,128)S(1)}, f32[32,128]{1,0:T(8,128)}, u32[]{:S(2)}) copy-start(f32[32,128]{1,0:T(8,128)} %param.14) | copy-start | bytes 49156
  5.7 21.3 %copy-start.2 = (bf16[2,64,4096]{1,0,2:T(2,128)(2,1)}, bf16[2,64,4096]{1,0,2:T(2,128)(2,1)S(1)}, u32[]{:S(2)}) copy-start(bf16[2,64,4096]{1,0,2:T(2,128)(2,1)S(1)} %copy.119) | copy-start | bytes 3145732
  8.5 0.6 copy-start.10
  27.0 46.0 %all-to-all-start = ((bf16[32,2,8192]{2,1,0:T(2,128)(2,1)}), bf16[32,2,8192]{2,1,0:T(2,128)(2,1)S(1)}, u32[]{:S(2)}, u32[]{:S(2)}) async-start(bf16[32,2,8192]{2,1,0:T(2,128)(2,1)} %reshape.147), calls=%async_computation | async-start | bytes 2097152 | tf_op jit(solution)/shard_map/all_to_all | solution.py:102
  41.6 1.3 copy-start.4
  42.9 5.1 copy-start.14
  43.7 0.6 copy-start.7
  73.0 30.6 %all-to-all-start.2 = ((bf16[32,2,8192]{2,1,0:T(2,128)(2,1)}), bf16[32,2,8192]{2,1,0:T(2,128)(2,1)}, u32[]{:S(2)}, u32[]{:S(2)}) async-start(bf16[32,2,8192]{2,1,0:T(2,128)(2,1)} %reshape.151), calls=%async_computation.2 | async-start | bytes 2097152 | tf_op jit(solution)/shard_map/all_to_all | solution.py:103
  103.6 29.2 %all-to-all-start.1 = ((bf16[32,2,8192]{2,1,0:T(2,128)(2,1)}), bf16[32,2,8192]{2,1,0:T(2,128)(2,1)}, u32[]{:S(2)}, u32[]{:S(2)}) async-start(bf16[32,2,8192]{2,1,0:T(2,128)(2,1)} %reshape.149), calls=%async_computation.1 | async-start | bytes 2097152 | tf_op jit(solution)/shard_map/all_to_all | solution.py:105
  132.8 29.2 %all-to-all-start.3 = ((bf16[32,2,8192]{2,1,0:T(2,128)(2,1)}), bf16[32,2,8192]{2,1,0:T(2,128)(2,1)}, u32[]{:S(2)}, u32[]{:S(2)}) async-start(bf16[32,2,8192]{2,1,0:T(2,128)(2,1)} %reshape.153), calls=%async_computation.3 | async-start | bytes 2097152 | tf_op jit(solution)/shard_map/all_to_all | solution.py:104
  177.6 1.9 copy-start
  180.3 3.7 copy-start.1
  180.4 3.7 copy-start.6
  190.5 1.9 copy-start
  193.2 3.7 copy-start.1
  193.3 3.7 copy-start.6
  203.4 1.9 copy-start
  206.2 3.7 copy-start.1
  206.2 3.7 copy-start.6
  216.3 1.9 copy-start
  219.1 3.7 copy-start.1
  219.1 3.7 copy-start.6
  238.1 1.9 copy-start
  240.9 3.7 copy-start.1
  240.9 3.7 copy-start.6
  251.0 1.9 copy-start
  253.8 3.7 copy-start.1
  253.8 3.7 copy-start.6
  263.9 1.9 copy-start
  266.7 3.7 copy-start.1
  266.7 3.7 copy-start.6
  276.8 1.9 copy-start
  279.6 3.7 copy-start.1
  279.6 3.7 copy-start.6
  291.9 14.3 %copy-start.9 = (bf16[2,2048,128]{1,2,0:T(8,128)(2,1)S(1)}, bf16[2,2048,128]{1,2,0:T(8,128)(2,1)}, u32[]{:S(2)}) copy-start(bf16[2,2048,128]{1,2,0:T(8,128)(2,1)} %get-tuple-element.94) | copy-start | bytes 3145732
  291.9 49.3 %copy-start.16 = (u32[256]{0:T(256)S(1)}, u32[256]{0:T(256)}, u32[]{:S(2)}) copy-start(u32[256]{0:T(256)} %constant.57) | copy-start | bytes 3076
  295.6 40.9 %all-to-all-start.4 = ((bf16[2,2048,128]{2,0,1:T(2,128)(2,1)}), bf16[2,2048,128]{2,0,1:T(2,128)(2,1)S(1)}, u32[]{:S(2)}, u32[]{:S(2)}) async-start(bf16[2,2048,128]{2,0,1:T(2,128)(2,1)} %copy.133), calls=%async_computation.4 | async-start | bytes 2097152 | tf_op jit(solution)/shard_map/all_to_all | solution.py:109
  308.2 41.0 %copy-start.3 = (bf16[2,64,4096]{1,0,2:T(2,128)(2,1)S(1)}, bf16[2,64,4096]{1,0,2:T(2,128)(2,1)}, u32[]{:S(2)}) copy-start(bf16[2,64,4096]{1,0,2:T(2,128)(2,1)} %copy-done.2) | copy-start | bytes 3145732
  308.2 41.0 %copy-start.11 = (f32[2,64,32]{1,0,2:T(2,128)S(1)}, f32[2,64,32]{1,0,2:T(2,128)}, u32[]{:S(2)}) copy-start(f32[2,64,32]{1,0,2:T(2,128)} %copy-done.10) | copy-start | bytes 49156
  308.2 41.0 %copy-start.13 = (f32[32,128]{1,0:T(8,128)S(1)}, f32[32,128]{1,0:T(8,128)}, u32[]{:S(2)}) copy-start(f32[32,128]{1,0:T(8,128)} %param.14) | copy-start | bytes 49156
  336.5 47.1 %all-to-all-start.5 = ((bf16[2,2048,128]{2,0,1:T(2,128)(2,1)}), bf16[2,2048,128]{2,0,1:T(2,128)(2,1)}, u32[]{:S(2)}, u32[]{:S(2)}) async-start(bf16[2,2048,128]{2,0,1:T(2,128)(2,1)} %copy.138), calls=%async_computation.5 | async-start | bytes 2097152 | tf_op jit(solution)/shard_map/all_to_all | solution.py:110
  383.6 270.7 %all-to-all-start.6 = ((bf16[2,2048,128]{2,0,1:T(2,128)(2,1)}), bf16[2,2048,128]{2,0,1:T(2,128)(2,1)}, u32[]{:S(2)}, u32[]{:S(2)}) async-start(bf16[2,2048,128]{2,0,1:T(2,128)(2,1)} %copy.143), calls=%async_computation.6 | async-start | bytes 2097152 | tf_op jit(solution)/shard_map/all_to_all | solution.py:111
  404.1 7.5 %copy-start.5 = (f32[16,8,32,128]{3,2,1,0:T(8,128)S(1)}, f32[16,8,32,128]{3,2,1,0:T(8,128)}, u32[]{:S(2)}) copy-start(f32[16,8,32,128]{3,2,1,0:T(8,128)} %copy-done.4) | copy-start | bytes 6291460
  404.1 7.5 %copy-start.8 = (f32[2,64,32]{2,1,0:T(8,128)S(1)}, f32[2,64,32]{2,1,0:T(8,128)}, u32[]{:S(2)}) copy-start(f32[2,64,32]{2,1,0:T(8,128)} %copy-done.7) | copy-start | bytes 49156
  404.1 7.5 %copy-start.15 = (f32[32,128]{1,0:T(8,128)S(1)}, f32[32,128]{1,0:T(8,128)}, u32[]{:S(2)}) copy-start(f32[32,128]{1,0:T(8,128)} %param.15) | copy-start | bytes 49156
where the time goes:
time: 662 us; the launch traced here: 657 us
  blocking collectives  235 us (35%)
  local copies, waits for them, and re-layouts  131 us (20%)
  other arithmetic  85.5 us (13%)
  waiting for transfers between devices  80.7 us (12%)
  matrix products  68.6 us (10%)
  starting transfers between devices  55 us (8%)
    unnamed x1, blocking collectives  225 us
    unnamed x42, local copies, waits for them, and re-layouts  49.4 us
    reduce_sum x2, other arithmetic, norm_back(): term = jnp.sum(grad_wide * unit, axis=tuple(range(unit.ndim - 2)))  35.7 us
    dot_general x8, matrix products, advance(): jnp.einsum('hqk,qhd->khd', probs_low, grad_part, preferred_element_type=j...  29.2 us
    all_to_all x1, waiting for transfers between devices, body(): lax.all_to_all(computed[0], 'seq', split_axis=1, concat_axis=2, tiled=True)  28.3 us
    all_to_all x1, waiting for transfers between devices, body(): lax.all_to_all(k_sent, 'seq', split_axis=2, concat_axis=1, tiled=True)  18.6 us
    dot_general x8, matrix products, advance(): jnp.einsum('qhd,khd->hqk', grad_part, value_rows, preferred_element_type=...  17.7 us
    all_to_all x1, waiting for transfers between devices, body(): lax.all_to_all(out_grad, 'seq', split_axis=2, concat_axis=1, tiled=True)  17 us
  transfers between devices with their start and end apart: 7, of which 5 were waited for; matrix products, arithmetic and copies ran while one was open for 18% of the time, Pallas kernels for 0%

commit v1 on v0

v1 whole, which is shorter than its diff:
```python
import functools, math
import jax, jax.numpy as jnp
from jax import lax
from jax.experimental import pallas as pl
from jax.experimental.pallas import tpu as pltpu

DEPTH = 128
SCALE = DEPTH ** -0.5
EXP_SCALE = SCALE * math.log2(math.e)
BQ = 256
CHUNK = 512
NT = (((1,), (1,)), ((), ()))
NN = (((1,), (0,)), ((), ()))


def dot(a, b, dims=NN):
    return lax.dot_general(a, b, dims, preferred_element_type=jnp.float32)


def unit_of(raw):
    wide = raw.astype(jnp.float32)
    rate = lax.rsqrt(jnp.mean(wide * wide, axis=-1, keepdims=True) + 1e-06)
    return wide * rate, rate


def normalize(raw_ref, gain, normed_ref, rows=256):
    @pl.loop(0, raw_ref.shape[0], step=rows)
    def _(r):
        at = pl.ds(pl.multiple_of(r, rows), rows)
        unit, _ = unit_of(raw_ref[at])
        normed_ref[at] = (unit * gain).astype(jnp.bfloat16)


def norm_back(raw, grad, gain):
    unit, rate = unit_of(raw)
    wide = grad.astype(jnp.float32)
    scaled = gain * wide
    inner = jnp.mean(scaled * unit, axis=-1, keepdims=True)
    return (rate * (scaled - unit * inner)).astype(jnp.bfloat16), jnp.sum(wide * unit, axis=0, keepdims=True)


def fold(x, op):
    rows = x.shape[0]
    out = x[:8]
    for r in range(8, rows, 8):
        out = op(out, x[r:r + 8])
    return out


def attend_block(qn, g, kn_ref, knt_ref, v_ref, w_ref, p_ref, key_acc, value_acc):
    length = kn_ref.shape[0]
    chunks = [pl.ds(c, CHUNK) for c in range(0, length, CHUNK)]
    top = None
    for at in chunks:
        s = dot(kn_ref[at], qn, NT)
        w_ref[at] = s
        part = fold(s, jnp.maximum)
        top = part if top is None else jnp.maximum(top, part)
    top = jnp.max(top, axis=0, keepdims=True) * EXP_SCALE
    total = dotted = None
    for at in chunks:
        w = jnp.exp2(w_ref[at] * EXP_SCALE - top)
        w_ref[at] = w
        p = dot(v_ref[at], g, NT)
        p_ref[at] = p
        a, b = fold(w, jnp.add), fold(w * p, jnp.add)
        total, dotted = (a, b) if total is None else (total + a, dotted + b)
    total = jnp.sum(total, axis=0, keepdims=True)
    dotted = jnp.sum(dotted, axis=0, keepdims=True)
    inverse = 1.0 / total
    row_dot = dotted * inverse
    query_t = None
    for at in chunks:
        probs = w_ref[at] * inverse
        value_acc[at] += dot(probs.astype(jnp.bfloat16), g)
        score_grad = (probs * (p_ref[at] - row_dot) * SCALE).astype(jnp.bfloat16)
        key_acc[at] += dot(score_grad, qn)
        part = dot(knt_ref[:, at], score_grad)
        query_t = part if query_t is None else query_t + part
    return query_t.T.astype(jnp.bfloat16)

from jax.sharding import PartitionSpec as P

MESH = pl.DeviceIdType.MESH
BACK_ROWS = 256


def kernel(
    seq, dps, factor,
    k_in, v_in, q_in, g_in, q_gain, k_gain,
    q_out, k_out, v_out, q_term, k_term,
    held, ready, qn, kn, knt, w, p, key_acc, value_acc, term, terms,
    there_send, there_recv, there_own, back_send, back_recv, back_own, term_send, term_recv,
):
    me, group = lax.axis_index("seq"), lax.axis_index("dp")
    ins, outs = (k_in, v_in, q_in, g_in), (q_out, k_out, v_out)
    samples, tokens, _ = q_in.shape
    length = seq * tokens
    mine = pl.ds(pl.multiple_of(me * tokens, tokens), tokens)
    my_columns = pl.ds(pl.multiple_of(me * DEPTH, DEPTH), DEPTH)

    def there(b, t, peer):
        return pltpu.make_async_remote_copy(
            src_ref=ins[t].at[b, :, pl.ds(pl.multiple_of(peer * DEPTH, DEPTH), DEPTH)],
            dst_ref=held.at[b, t, mine],
            send_sem=there_send.at[b, t], recv_sem=there_recv.at[b, t],
            device_id=(group, peer), device_id_type=MESH)

    def there_local(b, t):
        return pltpu.make_async_copy(ins[t].at[b, :, my_columns], held.at[b, t, mine], there_own.at[b, t])

    def there_all(b, t):
        rows = held.at[b, t, pl.ds(0, length - tokens)]
        return pltpu.make_async_remote_copy(
            src_ref=rows, dst_ref=rows, send_sem=there_send.at[b, t], recv_sem=there_recv.at[b, t],
            device_id=(group, me), device_id_type=MESH)

    def back(b, o, peer):
        return pltpu.make_async_remote_copy(
            src_ref=ready.at[b, o, pl.ds(pl.multiple_of(peer * tokens, tokens), tokens)],
            dst_ref=outs[o].at[b, :, my_columns],
            send_sem=back_send.at[b, o], recv_sem=back_recv.at[b, o],
            device_id=(group, peer), device_id_type=MESH)

    def back_local(b, o):
        return pltpu.make_async_copy(ready.at[b, o, mine], outs[o].at[b, :, my_columns], back_own.at[b, o])

    def back_all(b, o):
        rows = ready.at[b, o, pl.ds(0, length - tokens)]
        return pltpu.make_async_remote_copy(
            src_ref=rows, dst_ref=rows, send_sem=back_send.at[b, o], recv_sem=back_recv.at[b, o],
            device_id=(group, me), device_id_type=MESH)

    def send_back(b, o):
        back_local(b, o).start()

        @pl.loop(1, seq)
        def _(r):
            back(b, o, lax.rem(me + r, seq)).start()

    barrier = pltpu.get_barrier_semaphore()

    @pl.loop(1, seq)
    def _(r):
        pl.semaphore_signal(barrier, inc=1, device_id=(group, lax.rem(me + r, seq)), device_id_type=MESH)

    @pl.loop(1, dps)
    def _(r):
        pl.semaphore_signal(barrier, inc=1, device_id=(lax.rem(group + r, dps), me), device_id_type=MESH)

    for b in range(samples):
        for t in range(4):
            there_local(b, t).start()
    pl.semaphore_wait(barrier, seq + dps - 2)
    for b in range(samples):
        for t in range(4):
            @pl.loop(1, seq)
            def _(r):
                there(b, t, lax.rem(me + r, seq)).start()

    gain_q, gain_k = q_gain[pl.ds(me, 1)], k_gain[pl.ds(me, 1)]
    term[...] = jnp.zeros_like(term)
    for b in range(samples):
        for t in range(4):
            there_local(b, t).wait()
            there_all(b, t).wait_recv()
        keys, values, queries, grads = (held.at[b, t] for t in range(4))
        normalize(keys, gain_k, kn)
        normalize(queries, gain_q, qn)
        knt[...] = kn[...].T
        key_acc[...] = jnp.zeros_like(key_acc)
        value_acc[...] = jnp.zeros_like(value_acc)

        @pl.loop(0, length, step=BQ)
        def _(r):
            at = pl.ds(pl.multiple_of(r, BQ), BQ)
            grad = attend_block(qn[at], grads[at], kn, knt, values, w, p, key_acc, value_acc)
            result, part = norm_back(queries[at], grad, gain_q)
            ready[b, 0, at] = result
            term[0:1] += part

        send_back(b, 0)

        @pl.loop(0, length, step=BACK_ROWS)
        def _(r):
            at = pl.ds(pl.multiple_of(r, BACK_ROWS), BACK_ROWS)
            result, part = norm_back(keys[at], key_acc[at].astype(jnp.bfloat16), gain_k)
            ready[b, 1, at] = result
            term[1:2] += part
            ready[b, 2, at] = value_acc[at].astype(jnp.bfloat16)

        send_back(b, 1)
        send_back(b, 2)

    def share(r):
        return pltpu.make_async_remote_copy(
            src_ref=term, dst_ref=terms.at[r], send_sem=term_send.at[r], recv_sem=term_recv.at[r],
            device_id=(lax.rem(group + r, dps), me), device_id_type=MESH)

    for r in range(1, dps):
        share(r).start()
    for r in range(1, dps):
        share(r).wait()
    total = term[...]
    for r in range(1, dps):
        total += terms[r]
    q_term[...] = total[0:1] * factor
    k_term[...] = total[1:2] * factor
    for b in range(samples):
        for t in range(4):
            there_all(b, t).wait_send()
        for o in range(3):
            back_local(b, o).wait()
            back_all(b, o).wait()


def solution(mesh):
    seq, dps = mesh.shape["seq"], mesh.shape["dp"]

    def step(queries, keys, values, out_grad, q_gain, k_gain):
        samples, tokens, _ = queries.shape
        length = seq * tokens
        vmem, anywhere = pl.BlockSpec(memory_space=pltpu.VMEM), pl.BlockSpec(memory_space=pl.ANY)
        whole = jax.ShapeDtypeStruct(queries.shape, jnp.bfloat16)
        row = jax.ShapeDtypeStruct((1, DEPTH), jnp.float32)
        dma = pltpu.SemaphoreType.DMA
        return pl.pallas_call(
            functools.partial(kernel, seq, dps, 1.0 / math.sqrt(samples * dps * length)),
            out_shape=(whole, whole, whole, row, row),
            in_specs=[anywhere] * 4 + [vmem] * 2,
            out_specs=[anywhere] * 3 + [vmem] * 2,
            scratch_shapes=[
                pltpu.VMEM((samples, 4, length, DEPTH), jnp.bfloat16),
                pltpu.VMEM((samples, 3, length, DEPTH), jnp.bfloat16),
                pltpu.VMEM((length, DEPTH), jnp.bfloat16),
                pltpu.VMEM((length, DEPTH), jnp.bfloat16),
                pltpu.VMEM((DEPTH, length), jnp.bfloat16),
                pltpu.VMEM((length, BQ), jnp.float32),
                pltpu.VMEM((length, BQ), jnp.float32),
                pltpu.VMEM((length, DEPTH), jnp.float32),
                pltpu.VMEM((length, DEPTH), jnp.float32),
                pltpu.VMEM((8, DEPTH), jnp.float32),
                pltpu.VMEM((dps, 8, DEPTH), jnp.float32),
                dma((samples, 4)), dma((samples, 4)), dma((samples, 4)),
                dma((samples, 3)), dma((samples, 3)), dma((samples, 3)),
                dma((dps,)), dma((dps,)),
            ],
            compiler_params=pltpu.CompilerParams(
                collective_id=0, has_side_effects=True, vmem_limit_bytes=48 * 2**20
            ),
        )(keys, values, queries, out_grad, q_gain, k_gain)

    return jax.shard_map(
        step,
        mesh=mesh,
        in_specs=(P("dp", "seq", None),) * 4 + (P(), P()),
        out_specs=(P("dp", "seq", None),) * 3 + (P("seq", None),) * 2,
        check_vma=False,
    )
```

time: 662 us -> 183 us (0.28)
  blocking collectives: 235 us -> 0 us
  Pallas kernels: 0 us -> 172 us
  local copies, waits for them, and re-layouts: 131 us -> 7.81 us
  other arithmetic: 85.5 us -> 0 us
  waiting for transfers between devices: 80.7 us -> 0 us
  matrix products: 68.6 us -> 0 us
  starting transfers between devices: 55 us -> 0 us
    unnamed x1 -> x0, blocking collectives: 225 us -> none
    pallas_call x0 -> x1, Pallas kernels: none -> 172 us  [step(): pl.pallas_call(functools.partial(kernel, seq, dps, 1.0 / math.sqrt(sample...]
    all_to_all x7 -> x0, waiting for transfers between devices: 80.7 us -> none  [the longest x1 28.3 us: body(): lax.all_to_all(computed[0], 'seq', split_axis=1, concat_axis=2, tiled=True)]
    dot_general x40 -> x0, matrix products: 68.6 us -> none  [the longest x8 29.2 us: advance(): jnp.einsum('hqk,qhd->khd', probs_low, grad_part, preferred_element_type=j...]
    all_to_all x7 -> x0, starting transfers between devices: 55 us -> none  [the longest x1 13 us: body(): lax.all_to_all(q_sent, 'seq', split_axis=2, concat_axis=1, tiled=True)]
    reduce_sum x12 -> x0, other arithmetic: 45.5 us -> none  [the longest x2 35.7 us: norm_back(): term = jnp.sum(grad_wide * unit, axis=tuple(range(unit.ndim - 2)))]
    unnamed x42 -> x13, local copies, waits for them, and re-layouts: 49.4 us -> 7.81 us
    convert_element_type x12 -> x0, other arithmetic: 36.7 us -> none  [the longest x2 14.6 us: normalize(): return (unit, rate, (unit * gain).astype(jnp.bfloat16))]
  transfers between devices with their start and end apart: 7 -> 0, of which waited for: 5 -> 0; matrix products, arithmetic and copies ran while one was open for 18% -> 0% of each run, Pallas kernels for 0% -> 0%
where the time goes in v1:
time: 183 us; the launch traced here: 180 us
  Pallas kernels  172 us (94%)
  local copies, waits for them, and re-layouts  7.81 us (4%)
    pallas_call x1, Pallas kernels, step(): pl.pallas_call(functools.partial(kernel, seq, dps, 1.0 / math.sqrt(sample...  172 us
    unnamed x13, local copies, waits for them, and re-layouts  7.81 us

profile of v1, /device:TPU:32, one launch (start us, length us, event | category | flops | bytes accessed | tf_op | source)
XLA Modules:
  0.0 180.1 jit_solution(13949395892291237537)
XLA Ops:
  0.6 0.0 copy-start
  0.6 1.2 copy-done
  1.9 0.0 copy-start.1
  1.9 1.2 copy-done.1
  3.1 0.0 copy-start.2
  3.1 0.7 copy-done.2
  3.8 0.0 copy-start.3
  3.8 0.7 copy-done.3
  4.5 171.6 %shard_map.101 = (bf16[2,64,4096]{2,1,0:T(8,128)(2,1)S(1)}, bf16[2,64,4096]{2,1,0:T(8,128)(2,1)S(1)}, bf16[2,64,4096]{2,1,0:T(8,128)(2,1)S(1)}, f32[1,128]{1,0:T(1,128)S(1)}, f32[1,128]{1,0:T(1,128)S(1)}) custom-call(bf16[2,64,4096]{2,1,0:T(8,128)(2,1)S(1)} %copy-done, bf16[2,64,4096]{2,1,0:T(8,128)(2,1)S(1)} %copy-done.1, bf16[2,64,4096]{2,1,0:T(8,128)(2,1)} %q_in.1, ...), custom_call_target="tpu_custom_call" | custom-call | tf_op jit(solution)/shard_map/pallas_call | solution.py:227
  176.2 1.0 copy.16
  177.1 1.0 copy.17
  178.1 1.0 copy.18
  179.1 0.5 copy.19
  179.6 0.5 copy.20
Async XLA Ops:
  0.6 1.2 copy-start
  1.9 1.2 copy-start.1
  3.1 0.7 copy-start.2
  3.8 0.7 copy-start.3

commit v2 on v1

v2 whole, which is shorter than its diff:
```python
import functools, math
import jax, jax.numpy as jnp
from jax import lax
from jax.experimental import pallas as pl
from jax.experimental.pallas import tpu as pltpu

DEPTH = 128
SCALE = DEPTH ** -0.5
EXP_SCALE = SCALE * math.log2(math.e)
BQ = 256
CHUNK = 512
BLOCKS = 4
NT = (((1,), (1,)), ((), ()))
NN = (((1,), (0,)), ((), ()))


def dot(a, b, dims=NN):
    return lax.dot_general(a, b, dims, preferred_element_type=jnp.float32)


def unit_of(raw):
    wide = raw.astype(jnp.float32)
    rate = lax.rsqrt(jnp.mean(wide * wide, axis=-1, keepdims=True) + 1e-06)
    return wide * rate, rate


def normalize(raw_ref, gain, normed_ref, rows=256):
    @pl.loop(0, raw_ref.shape[0], step=rows)
    def _(r):
        at = pl.ds(pl.multiple_of(r, rows), rows)
        unit, _ = unit_of(raw_ref[at])
        normed_ref[at] = (unit * gain).astype(jnp.bfloat16)


def norm_back(raw, grad, gain):
    unit, rate = unit_of(raw)
    wide = grad.astype(jnp.float32)
    scaled = gain * wide
    inner = jnp.mean(scaled * unit, axis=-1, keepdims=True)
    return (rate * (scaled - unit * inner)).astype(jnp.bfloat16), jnp.sum(wide * unit, axis=0, keepdims=True)


def fold(x, op):
    rows = x.shape[0]
    out = x[:8]
    for r in range(8, rows, 8):
        out = op(out, x[r:r + 8])
    return out


from jax.sharding import PartitionSpec as P

MESH = pl.DeviceIdType.MESH


def weigh(qn, g, kn_ref, v_ref, w_ref, p_ref):
    chunks = [pl.ds(c, CHUNK) for c in range(0, kn_ref.shape[0], CHUNK)]
    top = None
    for at in chunks:
        s = dot(kn_ref[at], qn, NT)
        w_ref[at] = s
        part = fold(s, jnp.maximum)
        top = part if top is None else jnp.maximum(top, part)
    top = jnp.max(top, axis=0, keepdims=True) * EXP_SCALE
    total = dotted = None
    for at in chunks:
        w = jnp.exp2(w_ref[at] * EXP_SCALE - top)
        w_ref[at] = w
        p = dot(v_ref[at], g, NT)
        p_ref[at] = p
        a, b = fold(w, jnp.add), fold(w * p, jnp.add)
        total, dotted = (a, b) if total is None else (total + a, dotted + b)
    return top, jnp.sum(total, axis=0, keepdims=True), jnp.sum(dotted, axis=0, keepdims=True)


def gradients(qn, g, inverse, row_dot, knt_ref, w_ref, p_ref, key_acc, value_acc):
    query_t = None
    for c in range(0, w_ref.shape[0], CHUNK):
        at = pl.ds(c, CHUNK)
        probs = w_ref[at] * inverse
        value_acc[at] += dot(probs.astype(jnp.bfloat16), g)
        score_grad = (probs * (p_ref[at] - row_dot) * SCALE).astype(jnp.bfloat16)
        key_acc[at] += dot(score_grad, qn)
        part = dot(knt_ref[:, at], score_grad)
        query_t = part if query_t is None else query_t + part
    return query_t


def kernel(
    pairs, dps, factor,
    q_in, g_in, k_in, v_in, q_gain_in, k_gain_in,
    q_out, k_out, v_out, q_term, k_term,
    held, kept, ready, qn, kn, knt, w, p, key_acc, value_acc, own_part, part, their_part, stats, their_stats, term, terms,
    q_gain, k_gain, gain_sem, there_send, there_recv, kept_send, kept_recv, own_sem, back_send, back_recv, back_own,
    part_send, part_recv, stats_send, stats_recv, term_send, term_recv,
):
    me, group = lax.axis_index("seq"), lax.axis_index("dp")
    j, half = me // 2, lax.rem(me, 2)
    other = 1 - half
    ins, outs = (q_in, g_in, k_in, v_in), (q_out, k_out, v_out)
    samples, tokens, _ = q_in.shape
    items = 2 * samples
    length = pairs * tokens
    span = length // BLOCKS
    mine = pl.ds(pl.multiple_of(j * tokens, tokens), tokens)
    partner = (group, 2 * j + other)

    def columns(i, pair):
        return pl.ds(pl.multiple_of((2 * pair + i % 2) * DEPTH, DEPTH), DEPTH)

    def rows_of(pair):
        return pl.ds(pl.multiple_of(pair * tokens, tokens), tokens)

    def there(i, t, side, pair):
        return pltpu.make_async_remote_copy(
            src_ref=ins[t].at[i // 2, :, columns(i, pair)], dst_ref=held.at[i, t, side, mine],
            send_sem=there_send.at[i, t, side], recv_sem=there_recv.at[i, t, side],
            device_id=(group, 2 * pair + (other if side else half)), device_id_type=MESH)

    def keep(i, t, pair):
        return pltpu.make_async_remote_copy(
            src_ref=ins[t + 2].at[i // 2, :, columns(i, pair)], dst_ref=kept.at[i, t, mine],
            send_sem=kept_send.at[i, t], recv_sem=kept_recv.at[i, t],
            device_id=(group, 2 * pair + half), device_id_type=MESH)

    def own(i, t):
        target = held.at[i, t, 0, mine] if t < 2 else kept.at[i, t - 2, mine]
        return pltpu.make_async_copy(ins[t].at[i // 2, :, columns(i, j)], target, own_sem.at[i, t])

    def back(i, o, pair):
        return pltpu.make_async_remote_copy(
            src_ref=ready.at[i, o, rows_of(pair)], dst_ref=outs[o].at[i // 2, :, columns(i, j)],
            send_sem=back_send.at[i, o], recv_sem=back_recv.at[i, o],
            device_id=(group, 2 * pair + half), device_id_type=MESH)

    def back_local(i, o):
        return pltpu.make_async_copy(ready.at[i, o, mine], outs[o].at[i // 2, :, columns(i, j)], back_own.at[i, o])

    def all_of(send, recv, count):
        rows = held.at[0, 0, 0, pl.ds(0, count * tokens)]
        return pltpu.make_async_remote_copy(
            src_ref=rows, dst_ref=rows, send_sem=send, recv_sem=recv, device_id=(group, me), device_id_type=MESH)

    def there_all(i, t, side):
        return all_of(there_send.at[i, t, side], there_recv.at[i, t, side], pairs if side else pairs - 1)

    def kept_all(i, t):
        return all_of(kept_send.at[i, t], kept_recv.at[i, t], pairs - 1)

    def back_all(i, o):
        return all_of(back_send.at[i, o], back_recv.at[i, o], pairs - 1)

    def send_back(i, o):
        back_local(i, o).start()

        @pl.loop(1, pairs)
        def _(r):
            back(i, o, lax.rem(j + r, pairs)).start()

    def send_part(i, n):
        at = pl.ds(pl.multiple_of(n * span, span), span)
        return pltpu.make_async_remote_copy(
            src_ref=part.at[i, at], dst_ref=their_part.at[i, at],
            send_sem=part_send.at[i, n], recv_sem=part_recv.at[i, n], device_id=partner, device_id_type=MESH)

    def send_stats(i):
        return pltpu.make_async_remote_copy(
            src_ref=stats.at[i], dst_ref=their_stats.at[i],
            send_sem=stats_send.at[i], recv_sem=stats_recv.at[i], device_id=partner, device_id_type=MESH)

    def issue(i):
        for t in range(2):
            @pl.loop(0, pairs)
            def _(r):
                there(i, t, 1, lax.rem(j + r, pairs)).start()

        for t in range(2):
            @pl.loop(1, pairs)
            def _(r):
                keep(i, t, lax.rem(j + r, pairs)).start()

        for t in range(2):
            @pl.loop(1, pairs)
            def _(r):
                there(i, t, 0, lax.rem(j + r, pairs)).start()

    barrier = pltpu.get_barrier_semaphore()
    seq = 2 * pairs

    @pl.loop(1, seq)
    def _(r):
        pl.semaphore_signal(barrier, inc=1, device_id=(group, lax.rem(me + r, seq)), device_id_type=MESH)

    @pl.loop(1, dps)
    def _(r):
        for side in range(2):
            pl.semaphore_signal(
                barrier, inc=1, device_id=(lax.rem(group + r, dps), 2 * j + (other if side else half)),
                device_id_type=MESH)

    for i in range(items):
        for t in range(4):
            own(i, t).start()
    gains = [
        pltpu.make_async_copy(q_gain_in, q_gain, gain_sem.at[0]),
        pltpu.make_async_copy(k_gain_in, k_gain, gain_sem.at[1]),
    ]
    for copy in gains:
        copy.start()
    pl.semaphore_wait(barrier, seq - 1 + 2 * (dps - 1))
    issue(0)
    issue(1)

    for copy in gains:
        copy.wait()
    gain_q = [q_gain[pl.ds(2 * j + e, 1)] for e in range(2)]
    gain_k = [k_gain[pl.ds(2 * j + e, 1)] for e in range(2)]
    term[...] = jnp.zeros_like(term)

    def first(i, side):
        slot, e = i % 2, i % 2

        @pl.loop(0, BLOCKS)
        def _(block):
            n, at = side * BLOCKS + block, pl.ds(pl.multiple_of(block * span, span), span)
            unit, _ = unit_of(held[i, 0, side, at])
            normed = (unit * gain_q[e]).astype(jnp.bfloat16)
            qn[slot, side, at] = normed
            top, total, dotted = weigh(
                normed, held[i, 1, side, at], kn.at[slot], kept.at[i, 1], w.at[slot, n], p.at[slot, n])
            stats[i, 0, pl.ds(n, 1)] = top
            stats[i, 1, pl.ds(n, 1)] = total
            stats[i, 2, pl.ds(n, 1)] = dotted

    def near(i):
        slot, e = i % 2, i % 2
        own(i, 2).wait()
        kept_all(i, 0).wait_recv()
        normalize(kept.at[i, 0], gain_k[e], kn.at[slot])
        knt[slot] = kn[slot].T
        own(i, 3).wait()
        kept_all(i, 1).wait_recv()
        for t in range(2):
            own(i, t).wait()
            there_all(i, t, 0).wait_recv()
        first(i, 0)

    def send_parts(i):
        @pl.loop(0, BLOCKS)
        def _(n):
            send_part(i, n).start()

    def far(i):
        for t in range(2):
            there_all(i, t, 1).wait_recv()
        if i == items - 1:
            send_parts(0)
        first(i, 1)
        send_stats(i).start()
        if i + 2 < items:
            issue(i + 2)
        if i == items - 1:
            for past in range(1, items - 2):
                send_parts(past)

    def second(i):
        slot, e = i % 2, i % 2
        send_stats(i).wait_recv()
        key_acc[...] = jnp.zeros_like(key_acc)
        value_acc[...] = jnp.zeros_like(value_acc)

        @pl.loop(0, 2 * BLOCKS)
        def _(m):
            side, block = 1 - m // BLOCKS, lax.rem(m, BLOCKS)
            n, theirs = side * BLOCKS + block, (1 - side) * BLOCKS + block
            at = pl.ds(pl.multiple_of(block * span, span), span)
            top, total, dotted = (stats[i, c, pl.ds(n, 1)] for c in range(3))
            their_top, their_total, their_dotted = (their_stats[i, c, pl.ds(theirs, 1)] for c in range(3))
            highest = jnp.maximum(top, their_top)
            here, away = jnp.exp2(top - highest), jnp.exp2(their_top - highest)
            inverse = 1.0 / (total * here + their_total * away)
            row_dot = (dotted * here + their_dotted * away) * inverse
            grad = gradients(
                qn[slot, side, at], held[i, 1, side, at], here * inverse, row_dot,
                knt.at[slot], w.at[slot, n], p.at[slot, n], key_acc, value_acc).T

            @pl.when(side == 1)
            def _():
                part[i, at] = grad.astype(jnp.bfloat16)
                if i >= items - 2:
                    send_part(i, block).start()

            @pl.when(side == 0)
            def _():
                own_part[i, at] = grad

        @pl.loop(0, BLOCKS)
        def _(n):
            at = pl.ds(pl.multiple_of(n * span, span), span)
            result, sums = norm_back(kept[i, 0, at], key_acc[at].astype(jnp.bfloat16), gain_k[e])
            ready[i, 1, at] = result
            term[e, 1:2] += sums
            ready[i, 2, at] = value_acc[at].astype(jnp.bfloat16)

        send_back(i, 1)
        send_back(i, 2)

    def last(i):
        e = i % 2

        @pl.loop(0, BLOCKS)
        def _(n):
            at = pl.ds(pl.multiple_of(n * span, span), span)
            send_part(i, n).wait_recv()
            grad = (own_part[i, at] + their_part[i, at].astype(jnp.float32)).astype(jnp.bfloat16)
            result, sums = norm_back(held[i, 0, 0, at], grad, gain_q[e])
            ready[i, 0, at] = result
            term[e, 0:1] += sums
            shift = span // tokens

            @pl.loop(0, shift)
            def _(r):
                pair = n * shift + r

                @pl.when(pair != j)
                def _():
                    back(i, 0, pair).start()

                @pl.when(pair == j)
                def _():
                    back_local(i, 0).start()

    near(0)
    far(0)
    near(1)
    far(1)
    for i in range(2, items):
        second(i - 2)
        near(i)
        far(i)
    for i in range(items - 2, items):
        second(i)
    for i in range(items):
        last(i)

    def share(r, side):
        slot = 2 * r + side
        return pltpu.make_async_remote_copy(
            src_ref=term.at[other if side else half], dst_ref=terms.at[slot],
            send_sem=term_send.at[slot], recv_sem=term_recv.at[slot],
            device_id=(lax.rem(group + r, dps), 2 * j + (other if side else half)), device_id_type=MESH)

    shares = [(r, side) for r in range(dps) for side in range(2) if r or side]
    for r, side in shares:
        share(r, side).start()
    for r, side in shares:
        share(r, side).wait()
    total = term[half]
    for r, side in shares:
        total += terms[2 * r + side]
    q_term[...] = total[0:1] * factor
    k_term[...] = total[1:2] * factor
    for i in range(items):
        send_stats(i).wait_send()
        for n in range(BLOCKS):
            send_part(i, n).wait_send()
        for t in range(2):
            kept_all(i, t).wait_send()
            for side in range(2):
                there_all(i, t, side).wait_send()
        for o in range(3):
            back_local(i, o).wait()
            back_all(i, o).wait()


def solution(mesh):
    seq, dps = mesh.shape["seq"], mesh.shape["dp"]
    pairs = seq // 2

    def step(queries, keys, values, out_grad, q_gain, k_gain):
        samples, tokens, _ = queries.shape
        items, length = 2 * samples, pairs * tokens
        assert length == BLOCKS * BQ
        vmem, anywhere = pl.BlockSpec(memory_space=pltpu.VMEM), pl.BlockSpec(memory_space=pl.ANY)
        whole = jax.ShapeDtypeStruct(queries.shape, jnp.bfloat16)
        row = jax.ShapeDtypeStruct((1, DEPTH), jnp.float32)
        dma = pltpu.SemaphoreType.DMA
        low, wide = jnp.bfloat16, jnp.float32
        return pl.pallas_call(
            functools.partial(kernel, pairs, dps, 1.0 / math.sqrt(samples * dps * seq * tokens)),
            out_shape=(whole, whole, whole, row, row),
            in_specs=[pl.BlockSpec(memory_space=pltpu.HBM)] * 6,
            out_specs=[anywhere] * 3 + [vmem] * 2,
            scratch_shapes=[
                pltpu.VMEM((items, 2, 2, length, DEPTH), low),
                pltpu.VMEM((items, 2, length, DEPTH), low),
                pltpu.VMEM((items, 3, length, DEPTH), low),
                pltpu.VMEM((2, 2, length, DEPTH), low),
                pltpu.VMEM((2, length, DEPTH), low),
                pltpu.VMEM((2, DEPTH, length), low),
                pltpu.VMEM((2, 2 * BLOCKS, length, BQ), wide),
                pltpu.VMEM((2, 2 * BLOCKS, length, BQ), wide),
                pltpu.VMEM((length, DEPTH), wide),
                pltpu.VMEM((length, DEPTH), wide),
                pltpu.VMEM((items, length, DEPTH), wide),
                pltpu.VMEM((items, length, DEPTH), low),
                pltpu.VMEM((items, length, DEPTH), low),
                pltpu.VMEM((items, 3, 2 * BLOCKS, BQ), wide),
                pltpu.VMEM((items, 3, 2 * BLOCKS, BQ), wide),
                pltpu.VMEM((2, 8, DEPTH), wide),
                pltpu.VMEM((2 * dps, 8, DEPTH), wide),
                pltpu.VMEM(q_gain.shape, wide), pltpu.VMEM(k_gain.shape, wide), dma((2,)),
                dma((items, 2, 2)), dma((items, 2, 2)), dma((items, 2)), dma((items, 2)), dma((items, 4)),
                dma((items, 3)), dma((items, 3)), dma((items, 3)),
                dma((items, BLOCKS)), dma((items, BLOCKS)), dma((items,)), dma((items,)),
                dma((2 * dps,)), dma((2 * dps,)),
            ],
            compiler_params=pltpu.CompilerParams(
                collective_id=0, has_side_effects=True, vmem_limit_bytes=60 * 2**20
            ),
        )(queries, out_grad, keys, values, q_gain, k_gain)

    return jax.shard_map(
        step,
        mesh=mesh,
        in_specs=(P("dp", "seq", None),) * 4 + (P(), P()),
        out_specs=(P("dp", "seq", None),) * 3 + (P("seq", None),) * 2,
        check_vma=False,
    )
```

time: 183 us -> 175 us (0.956); the launches traced: 180 us -> 174 us
  Pallas kernels: 172 us -> 168 us
    pallas_call x1, Pallas kernels: 172 us -> 168 us  [step(): pl.pallas_call(functools.partial(kernel, pairs, dps, 1.0 / math.sqrt(samp...]
where the time goes in v2:
time: 175 us; the launch traced here: 174 us
  Pallas kernels  168 us (96%)
  local copies, waits for them, and re-layouts  6.14 us (4%)
    pallas_call x1, Pallas kernels, step(): pl.pallas_call(functools.partial(kernel, pairs, dps, 1.0 / math.sqrt(samp...  168 us
    unnamed x13, local copies, waits for them, and re-layouts  6.14 us

profile of v2, /device:TPU:32, one launch (start us, length us, event | category | flops | bytes accessed | tf_op | source)
XLA Modules:
  0.0 174.4 jit_solution(12823853999756154695)
XLA Ops:
  0.6 167.7 %shard_map.101 = (bf16[2,64,4096]{2,1,0:T(8,128)(2,1)}, bf16[2,64,4096]{2,1,0:T(8,128)(2,1)}, bf16[2,64,4096]{2,1,0:T(8,128)(2,1)}, f32[1,128]{1,0:T(1,128)}, f32[1,128]{1,0:T(1,128)}) custom-call(bf16[2,64,4096]{2,1,0:T(8,128)(2,1)} %q_in.1, bf16[2,64,4096]{2,1,0:T(8,128)(2,1)} %g_in.1, bf16[2,64,4096]{2,1,0:T(8,128)(2,1)} %k_in.1, ...), custom_call_target="tpu_custom_call" | custom-call | tf_op jit(solution)/shard_map/pallas_call | solution.py:389
  168.3 0.0 copy-start.1
  168.3 2.4 %copy.16 = bf16[2,64,4096]{2,1,0:T(8,128)(2,1)} copy(bf16[2,64,4096]{2,1,0:T(8,128)(2,1)} %get-tuple-element.10) | data formatting | bytes 2097152
  170.7 0.0 copy-done.1
  170.7 0.0 copy-start
  170.7 1.0 copy.17
  171.7 0.6 copy-done
  172.3 0.0 copy-start.3
  172.3 1.0 copy.18
  173.3 0.0 copy-done.3
  173.3 0.0 copy-start.2
  173.3 0.5 copy.19
  173.8 0.2 copy-done.2
  173.9 0.5 copy.20
Async XLA Ops:
  168.3 2.4 %copy-start.1 = (bf16[2,64,4096]{2,1,0:T(8,128)(2,1)S(1)}, bf16[2,64,4096]{2,1,0:T(8,128)(2,1)}, u32[]{:S(2)}) copy-start(bf16[2,64,4096]{2,1,0:T(8,128)(2,1)} %get-tuple-element.11) | copy-start | bytes 3145732
  170.7 1.6 copy-start
  172.3 1.0 copy-start.3
  173.3 0.7 copy-start.2

commit v3 on v2

--- a/solution.py
+++ b/solution.py
@@ -90,9 +90,9 @@
     pairs, dps, factor,
     q_in, g_in, k_in, v_in, q_gain_in, k_gain_in,
     q_out, k_out, v_out, q_term, k_term,
-    held, kept, ready, qn, kn, knt, w, p, key_acc, value_acc, own_part, part, their_part, stats, their_stats, term, terms,
+    held, kept, ready, qn, kn, knt, w, p, key_acc, value_acc, own_part, part, their_part, tops, stats, their_stats, own_center, their_center, center_t, term, terms,
     q_gain, k_gain, gain_sem, there_send, there_recv, kept_send, kept_recv, own_sem, back_send, back_recv, back_own,
-    part_send, part_recv, stats_send, stats_recv, term_send, term_recv,
+    part_send, part_recv, stats_send, stats_recv, center_send, center_recv, term_send, term_recv,
 ):
     me, group = lax.axis_index("seq"), lax.axis_index("dp")
     j, half = me // 2, lax.rem(me, 2)
@@ -167,6 +167,11 @@
         return pltpu.make_async_remote_copy(
             src_ref=stats.at[i], dst_ref=their_stats.at[i],
             send_sem=stats_send.at[i], recv_sem=stats_recv.at[i], device_id=partner, device_id_type=MESH)
+
+    def send_center(i):
+        return pltpu.make_async_remote_copy(
+            src_ref=own_center.at[i], dst_ref=their_center.at[i],
+            send_sem=center_send.at[i], recv_sem=center_recv.at[i], device_id=partner, device_id_type=MESH)
 
     def issue(i):
         for t in range(2):
@@ -228,9 +233,9 @@
             qn[slot, side, at] = normed
             top, total, dotted = weigh(
                 normed, held[i, 1, side, at], kn.at[slot], kept.at[i, 1], w.at[slot, n], p.at[slot, n])
-            stats[i, 0, pl.ds(n, 1)] = top
-            stats[i, 1, pl.ds(n, 1)] = total
-            stats[i, 2, pl.ds(n, 1)] = dotted
+            tops[slot, pl.ds(n, 1)] = top
+            stats[i, 0, pl.ds(n, 1)] = top + jnp.log2(total)
+            stats[i, 1, pl.ds(n, 1)] = dotted / total
 
     def near(i):
         slot, e = i % 2, i % 2
@@ -238,6 +243,9 @@
         kept_all(i, 0).wait_recv()
         normalize(kept.at[i, 0], gain_k[e], kn.at[slot])
         knt[slot] = kn[slot].T
+        mean = jnp.mean(kn[slot].astype(jnp.float32), axis=0, keepdims=True)
+        own_center[i] = jnp.broadcast_to(mean, (8, DEPTH))
+        send_center(i).start()
         own(i, 3).wait()
         kept_all(i, 1).wait_recv()
         for t in range(2):
@@ -266,6 +274,9 @@
     def second(i):
         slot, e = i % 2, i % 2
         send_stats(i).wait_recv()
+        send_center(i).wait_recv()
+        for side, center in enumerate((their_center, own_center)):
+            center_t[side] = jnp.broadcast_to(center[i, 0:1], (BQ, DEPTH)).T
         key_acc[...] = jnp.zeros_like(key_acc)
         value_acc[...] = jnp.zeros_like(value_acc)
 
@@ -274,15 +285,21 @@
             side, block = 1 - m // BLOCKS, lax.rem(m, BLOCKS)
             n, theirs = side * BLOCKS + block, (1 - side) * BLOCKS + block
             at = pl.ds(pl.multiple_of(block * span, span), span)
-            top, total, dotted = (stats[i, c, pl.ds(n, 1)] for c in range(3))
-            their_top, their_total, their_dotted = (their_stats[i, c, pl.ds(theirs, 1)] for c in range(3))
-            highest = jnp.maximum(top, their_top)
-            here, away = jnp.exp2(top - highest), jnp.exp2(their_top - highest)
-            inverse = 1.0 / (total * here + their_total * away)
+            level, dotted = (stats[i, c, pl.ds(n, 1)] for c in range(2))
+            their_level, their_dotted = (their_stats[i, c, pl.ds(theirs, 1)] for c in range(2))
+            highest = jnp.maximum(level, their_level)
+            here, away = jnp.exp2(level - highest), jnp.exp2(their_level - highest)
+            inverse = 1.0 / (here + away)
             row_dot = (dotted * here + their_dotted * away) * inverse
+            scale = jnp.exp2(tops[slot, pl.ds(n, 1)] - highest) * inverse
+            gone = here * inverse * (row_dot - dotted) * SCALE
+            back_in = away * inverse * (their_dotted - row_dot) * SCALE
             grad = gradients(
-                qn[slot, side, at], held[i, 1, side, at], here * inverse, row_dot,
-                knt.at[slot], w.at[slot, n], p.at[slot, n], key_acc, value_acc).T
+                qn[slot, side, at], held[i, 1, side, at], scale, row_dot,
+                knt.at[slot], w.at[slot, n], p.at[slot, n], key_acc, value_acc)
+            grad = (grad + center_t[side] * jnp.where(side == 1, gone, back_in)).T
+            unit, _ = unit_of(held[i, 0, side, at])
+            term[e, 0:1] += jnp.sum(grad * unit, axis=0, keepdims=True)
 
             @pl.when(side == 1)
             def _():
@@ -313,9 +330,7 @@
             at = pl.ds(pl.multiple_of(n * span, span), span)
             send_part(i, n).wait_recv()
             grad = (own_part[i, at] + their_part[i, at].astype(jnp.float32)).astype(jnp.bfloat16)
-            result, sums = norm_back(held[i, 0, 0, at], grad, gain_q[e])
-            ready[i, 0, at] = result
-            term[e, 0:1] += sums
+            ready[i, 0, at], _ = norm_back(held[i, 0, 0, at], grad, gain_q[e])
             shift = span // tokens
 
             @pl.loop(0, shift)
@@ -340,9 +355,6 @@
         far(i)
     for i in range(items - 2, items):
         second(i)
-    for i in range(items):
-        last(i)
-
     def share(r, side):
         slot = 2 * r + side
         return pltpu.make_async_remote_copy(
@@ -353,6 +365,8 @@
     shares = [(r, side) for r in range(dps) for side in range(2) if r or side]
     for r, side in shares:
         share(r, side).start()
+    for i in range(items):
+        last(i)
     for r, side in shares:
         share(r, side).wait()
     total = term[half]
@@ -362,6 +376,7 @@
     k_term[...] = total[1:2] * factor
     for i in range(items):
         send_stats(i).wait_send()
+        send_center(i).wait_send()
         for n in range(BLOCKS):
             send_part(i, n).wait_send()
         for t in range(2):
@@ -373,6 +388,15 @@
             back_all(i, o).wait()
 
 
+def hand_over(*refs):
+    sems = refs[-1]
+    copies = [pltpu.make_async_copy(src, dst, sems.at[c]) for c, (src, dst) in enumerate(zip(refs[:5], refs[5:10]))]
+    for copy in copies:
+        copy.start()
+    for copy in copies:
+        copy.wait()
+
+
 def solution(mesh):
     seq, dps = mesh.shape["seq"], mesh.shape["dp"]
     pairs = seq // 2
@@ -381,16 +405,16 @@
         samples, tokens, _ = queries.shape
         items, length = 2 * samples, pairs * tokens
         assert length == BLOCKS * BQ
-        vmem, anywhere = pl.BlockSpec(memory_space=pltpu.VMEM), pl.BlockSpec(memory_space=pl.ANY)
+        vmem = pl.BlockSpec(memory_space=pltpu.VMEM)
         whole = jax.ShapeDtypeStruct(queries.shape, jnp.bfloat16)
         row = jax.ShapeDtypeStruct((1, DEPTH), jnp.float32)
         dma = pltpu.SemaphoreType.DMA
         low, wide = jnp.bfloat16, jnp.float32
-        return pl.pallas_call(
+        results = pl.pallas_call(
             functools.partial(kernel, pairs, dps, 1.0 / math.sqrt(samples * dps * seq * tokens)),
-            out_shape=(whole, whole, whole, row, row),
+            out_shape=(pltpu.VMEM(whole.shape, low),) * 3 + (pltpu.VMEM(row.shape, wide),) * 2,
             in_specs=[pl.BlockSpec(memory_space=pltpu.HBM)] * 6,
-            out_specs=[anywhere] * 3 + [vmem] * 2,
+            out_specs=[vmem] * 5,
             scratch_shapes=[
                 pltpu.VMEM((items, 2, 2, length, DEPTH), low),
                 pltpu.VMEM((items, 2, length, DEPTH), low),
@@ -405,20 +429,32 @@
                 pltpu.VMEM((items, length, DEPTH), wide),
                 pltpu.VMEM((items, length, DEPTH), low),
                 pltpu.VMEM((items, length, DEPTH), low),
-                pltpu.VMEM((items, 3, 2 * BLOCKS, BQ), wide),
-                pltpu.VMEM((items, 3, 2 * BLOCKS, BQ), wide),
+                pltpu.VMEM((2, 2 * BLOCKS, BQ), wide),
+                pltpu.VMEM((items, 2, 2 * BLOCKS, BQ), wide),
+                pltpu.VMEM((items, 2, 2 * BLOCKS, BQ), wide),
+                pltpu.VMEM((items, 8, DEPTH), wide),
+                pltpu.VMEM((items, 8, DEPTH), wide),
+                pltpu.VMEM((2, DEPTH, BQ), wide),
                 pltpu.VMEM((2, 8, DEPTH), wide),
                 pltpu.VMEM((2 * dps, 8, DEPTH), wide),
                 pltpu.VMEM(q_gain.shape, wide), pltpu.VMEM(k_gain.shape, wide), dma((2,)),
                 dma((items, 2, 2)), dma((items, 2, 2)), dma((items, 2)), dma((items, 2)), dma((items, 4)),
                 dma((items, 3)), dma((items, 3)), dma((items, 3)),
-                dma((items, BLOCKS)), dma((items, BLOCKS)), dma((items,)), dma((items,)),
+                dma((items, BLOCKS)), dma((items, BLOCKS)), dma((items,)), dma((items,)), dma((items,)), dma((items,)),
                 dma((2 * dps,)), dma((2 * dps,)),
             ],
             compiler_params=pltpu.CompilerParams(
-                collective_id=0, has_side_effects=True, vmem_limit_bytes=60 * 2**20
+                collective_id=0, has_side_effects=True, vmem_limit_bytes=52 * 2**20
             ),
         )(queries, out_grad, keys, values, q_gain, k_gain)
+        hbm = pl.BlockSpec(memory_space=pltpu.HBM)
+        return pl.pallas_call(
+            hand_over,
+            out_shape=(pltpu.HBM(whole.shape, low),) * 3 + (pltpu.HBM(row.shape, wide),) * 2,
+            in_specs=[vmem] * 5,
+            out_specs=[hbm] * 5,
+            scratch_shapes=[dma((5,))],
+        )(*(pltpu.with_memory_space_constraint(x, pltpu.VMEM) for x in results))
 
     return jax.shard_map(
         step,

time: 175 us -> 169 us (0.966)
  local copies, waits for them, and re-layouts: 6.14 us -> 0 us
    unnamed x13 -> x0, local copies, waits for them, and re-layouts: 6.14 us -> none
where the time goes in v3:
time: 169 us
  Pallas kernels  168 us (99%)
    pallas_call x1, Pallas kernels, step(): pl.pallas_call(functools.partial(kernel, pairs, dps, 1.0 / math.sqrt(samp...  166 us

profile of v3, /device:TPU:32, one launch (start us, length us, event | category | flops | bytes accessed | tf_op | source)
XLA Modules:
  0.0 168.7 jit_solution(14828430281066450704)
XLA Ops:
  0.6 166.3 %shard_map.101 = (bf16[2,64,4096]{2,1,0:T(8,128)(2,1)S(1)}, bf16[2,64,4096]{2,1,0:T(8,128)(2,1)S(1)}, bf16[2,64,4096]{2,1,0:T(8,128)(2,1)S(1)}, f32[1,128]{1,0:T(1,128)S(1)}, f32[1,128]{1,0:T(1,128)S(1)}) custom-call(bf16[2,64,4096]{2,1,0:T(8,128)(2,1)} %q_in.1, bf16[2,64,4096]{2,1,0:T(8,128)(2,1)} %g_in.1, bf16[2,64,4096]{2,1,0:T(8,128)(2,1)} %k_in.1, ...), custom_call_target="tpu_custom_call" | custom-call | tf_op jit(solution)/shard_map/pallas_call | solution.py:413
  167.0 1.7 %shard_map.102 = (bf16[2,64,4096]{2,1,0:T(8,128)(2,1)}, bf16[2,64,4096]{2,1,0:T(8,128)(2,1)}, bf16[2,64,4096]{2,1,0:T(8,128)(2,1)}, f32[1,128]{1,0:T(1,128)}, f32[1,128]{1,0:T(1,128)}) custom-call(bf16[2,64,4096]{2,1,0:T(8,128)(2,1)S(1)} %get-tuple-element.10.refs_0_, bf16[2,64,4096]{2,1,0:T(8,128)(2,1)S(1)} %get-tuple-element.11.refs_1_, ...), custom_call_target="tpu_custom_call" | custom-call | tf_op jit(solution)/shard_map/pallas_call | solution.py:451

commit v4 on v3

--- a/solution.py
+++ b/solution.py
@@ -90,13 +90,14 @@
     pairs, dps, factor,
     q_in, g_in, k_in, v_in, q_gain_in, k_gain_in,
     q_out, k_out, v_out, q_term, k_term,
-    held, kept, ready, qn, kn, knt, w, p, key_acc, value_acc, own_part, part, their_part, tops, stats, their_stats, own_center, their_center, center_t, term, terms,
+    held, kept, ready, units, qn, kn, knt, w, p, key_acc, value_acc, own_part, part, their_part, tops, stats, their_stats, own_center, their_center, center_t, term, terms,
     q_gain, k_gain, gain_sem, there_send, there_recv, kept_send, kept_recv, own_sem, back_send, back_recv, back_own,
     part_send, part_recv, stats_send, stats_recv, center_send, center_recv, term_send, term_recv,
 ):
     me, group = lax.axis_index("seq"), lax.axis_index("dp")
     j, half = me // 2, lax.rem(me, 2)
     other = 1 - half
+    turn = j // (pairs // BLOCKS)
     ins, outs = (q_in, g_in, k_in, v_in), (q_out, k_out, v_out)
     samples, tokens, _ = q_in.shape
     items = 2 * samples
@@ -215,6 +216,7 @@
     pl.semaphore_wait(barrier, seq - 1 + 2 * (dps - 1))
     issue(0)
     issue(1)
+    issue(2)
 
     for copy in gains:
         copy.wait()
@@ -229,6 +231,7 @@
         def _(block):
             n, at = side * BLOCKS + block, pl.ds(pl.multiple_of(block * span, span), span)
             unit, _ = unit_of(held[i, 0, side, at])
+            units[slot, side, at] = unit
             normed = (unit * gain_q[e]).astype(jnp.bfloat16)
             qn[slot, side, at] = normed
             top, total, dotted = weigh(
@@ -244,7 +247,7 @@
         normalize(kept.at[i, 0], gain_k[e], kn.at[slot])
         knt[slot] = kn[slot].T
         mean = jnp.mean(kn[slot].astype(jnp.float32), axis=0, keepdims=True)
-        own_center[i] = jnp.broadcast_to(mean, (8, DEPTH))
+        own_center[i] = mean
         send_center(i).start()
         own(i, 3).wait()
         kept_all(i, 1).wait_recv()
@@ -256,17 +259,15 @@
     def send_parts(i):
         @pl.loop(0, BLOCKS)
         def _(n):
-            send_part(i, n).start()
+            send_part(i, lax.rem(n + turn, BLOCKS)).start()
 
     def far(i):
         for t in range(2):
             there_all(i, t, 1).wait_recv()
-        if i == items - 1:
-            send_parts(0)
         first(i, 1)
         send_stats(i).start()
-        if i + 2 < items:
-            issue(i + 2)
+        if i + 3 < items:
+            issue(i + 3)
         if i == items - 1:
             for past in range(1, items - 2):
                 send_parts(past)
@@ -276,13 +277,13 @@
         send_stats(i).wait_recv()
         send_center(i).wait_recv()
         for side, center in enumerate((their_center, own_center)):
-            center_t[side] = jnp.broadcast_to(center[i, 0:1], (BQ, DEPTH)).T
+            center_t[side] = jnp.broadcast_to(center[i], (BQ, DEPTH)).T
         key_acc[...] = jnp.zeros_like(key_acc)
         value_acc[...] = jnp.zeros_like(value_acc)
 
         @pl.loop(0, 2 * BLOCKS)
         def _(m):
-            side, block = 1 - m // BLOCKS, lax.rem(m, BLOCKS)
+            side, block = 1 - m // BLOCKS, lax.rem(m + turn, BLOCKS)
             n, theirs = side * BLOCKS + block, (1 - side) * BLOCKS + block
             at = pl.ds(pl.multiple_of(block * span, span), span)
             level, dotted = (stats[i, c, pl.ds(n, 1)] for c in range(2))
@@ -298,13 +299,12 @@
                 qn[slot, side, at], held[i, 1, side, at], scale, row_dot,
                 knt.at[slot], w.at[slot, n], p.at[slot, n], key_acc, value_acc)
             grad = (grad + center_t[side] * jnp.where(side == 1, gone, back_in)).T
-            unit, _ = unit_of(held[i, 0, side, at])
-            term[e, 0:1] += jnp.sum(grad * unit, axis=0, keepdims=True)
+            term[e, 0:1] += jnp.sum(grad * units[slot, side, at], axis=0, keepdims=True)
 
             @pl.when(side == 1)
             def _():
                 part[i, at] = grad.astype(jnp.bfloat16)
-                if i >= items - 2:
+                if i != 1:
                     send_part(i, block).start()
 
             @pl.when(side == 0)
@@ -326,7 +326,8 @@
         e = i % 2
 
         @pl.loop(0, BLOCKS)
-        def _(n):
+        def _(m):
+            n = lax.rem(m + turn, BLOCKS)
             at = pl.ds(pl.multiple_of(n * span, span), span)
             send_part(i, n).wait_recv()
             grad = (own_part[i, at] + their_part[i, at].astype(jnp.float32)).astype(jnp.bfloat16)
@@ -353,8 +354,9 @@
         second(i - 2)
         near(i)
         far(i)
-    for i in range(items - 2, items):
-        second(i)
+    second(items - 2)
+    last(0)
+    second(items - 1)
     def share(r, side):
         slot = 2 * r + side
         return pltpu.make_async_remote_copy(
@@ -365,7 +367,7 @@
     shares = [(r, side) for r in range(dps) for side in range(2) if r or side]
     for r, side in shares:
         share(r, side).start()
-    for i in range(items):
+    for i in range(1, items):
         last(i)
     for r, side in shares:
         share(r, side).wait()
@@ -419,6 +421,7 @@
                 pltpu.VMEM((items, 2, 2, length, DEPTH), low),
                 pltpu.VMEM((items, 2, length, DEPTH), low),
                 pltpu.VMEM((items, 3, length, DEPTH), low),
+                pltpu.VMEM((2, 2, length, DEPTH), wide),
                 pltpu.VMEM((2, 2, length, DEPTH), low),
                 pltpu.VMEM((2, length, DEPTH), low),
                 pltpu.VMEM((2, DEPTH, length), low),
@@ -432,11 +435,11 @@
                 pltpu.VMEM((2, 2 * BLOCKS, BQ), wide),
                 pltpu.VMEM((items, 2, 2 * BLOCKS, BQ), wide),
                 pltpu.VMEM((items, 2, 2 * BLOCKS, BQ), wide),
-                pltpu.VMEM((items, 8, DEPTH), wide),
-                pltpu.VMEM((items, 8, DEPTH), wide),
+                pltpu.VMEM((items, 1, DEPTH), wide),
+                pltpu.VMEM((items, 1, DEPTH), wide),
                 pltpu.VMEM((2, DEPTH, BQ), wide),
-                pltpu.VMEM((2, 8, DEPTH), wide),
-                pltpu.VMEM((2 * dps, 8, DEPTH), wide),
+                pltpu.VMEM((2, 2, DEPTH), wide),
+                pltpu.VMEM((2 * dps, 2, DEPTH), wide),
                 pltpu.VMEM(q_gain.shape, wide), pltpu.VMEM(k_gain.shape, wide), dma((2,)),
                 dma((items, 2, 2)), dma((items, 2, 2)), dma((items, 2)), dma((items, 2)), dma((items, 4)),
                 dma((items, 3)), dma((items, 3)), dma((items, 3)),
@@ -444,7 +447,7 @@
                 dma((2 * dps,)), dma((2 * dps,)),
             ],
             compiler_params=pltpu.CompilerParams(
-                collective_id=0, has_side_effects=True, vmem_limit_bytes=52 * 2**20
+                collective_id=0, has_side_effects=True, vmem_limit_bytes=54 * 2**20
             ),
         )(queries, out_grad, keys, values, q_gain, k_gain)
         hbm = pl.BlockSpec(memory_space=pltpu.HBM)

time: 169 us -> 165 us (0.976)
  Pallas kernels: 168 us -> 163 us
    pallas_call x1, Pallas kernels: 166 us -> 161 us  [step(): pl.pallas_call(functools.partial(kernel, pairs, dps, 1.0 / math.sqrt(samp...]
where the time goes in v4:
time: 165 us; the launch traced here: 164 us
  Pallas kernels  163 us (99%)
    pallas_call x1, Pallas kernels, step(): pl.pallas_call(functools.partial(kernel, pairs, dps, 1.0 / math.sqrt(samp...  161 us

profile of v4, /device:TPU:32, one launch (start us, length us, event | category | flops | bytes accessed | tf_op | source)
XLA Modules:
  0.0 163.7 jit_solution(12250740406342088286)
XLA Ops:
  0.6 161.3 %shard_map.101 = (bf16[2,64,4096]{2,1,0:T(8,128)(2,1)S(1)}, bf16[2,64,4096]{2,1,0:T(8,128)(2,1)S(1)}, bf16[2,64,4096]{2,1,0:T(8,128)(2,1)S(1)}, f32[1,128]{1,0:T(1,128)S(1)}, f32[1,128]{1,0:T(1,128)S(1)}) custom-call(bf16[2,64,4096]{2,1,0:T(8,128)(2,1)} %q_in.1, bf16[2,64,4096]{2,1,0:T(8,128)(2,1)} %g_in.1, bf16[2,64,4096]{2,1,0:T(8,128)(2,1)} %k_in.1, ...), custom_call_target="tpu_custom_call" | custom-call | tf_op jit(solution)/shard_map/pallas_call | solution.py:415
  162.0 1.7 %shard_map.102 = (bf16[2,64,4096]{2,1,0:T(8,128)(2,1)}, bf16[2,64,4096]{2,1,0:T(8,128)(2,1)}, bf16[2,64,4096]{2,1,0:T(8,128)(2,1)}, f32[1,128]{1,0:T(1,128)}, f32[1,128]{1,0:T(1,128)}) custom-call(bf16[2,64,4096]{2,1,0:T(8,128)(2,1)S(1)} %get-tuple-element.10.refs_0_, bf16[2,64,4096]{2,1,0:T(8,128)(2,1)S(1)} %get-tuple-element.11.refs_1_, ...), custom_call_target="tpu_custom_call" | custom-call | tf_op jit(solution)/shard_map/pallas_call | solution.py:454

commit v5 on v4

--- a/solution.py
+++ b/solution.py
@@ -154,7 +154,7 @@
     def send_back(i, o):
         back_local(i, o).start()
 
-        @pl.loop(1, pairs)
+        @pl.loop(1, pairs, unroll=5)
         def _(r):
             back(i, o, lax.rem(j + r, pairs)).start()
 
@@ -176,28 +176,28 @@
 
     def issue(i):
         for t in range(2):
-            @pl.loop(0, pairs)
+            @pl.loop(0, pairs, unroll=4)
             def _(r):
                 there(i, t, 1, lax.rem(j + r, pairs)).start()
 
         for t in range(2):
-            @pl.loop(1, pairs)
+            @pl.loop(1, pairs, unroll=5)
             def _(r):
                 keep(i, t, lax.rem(j + r, pairs)).start()
 
         for t in range(2):
-            @pl.loop(1, pairs)
+            @pl.loop(1, pairs, unroll=5)
             def _(r):
                 there(i, t, 0, lax.rem(j + r, pairs)).start()
 
     barrier = pltpu.get_barrier_semaphore()
     seq = 2 * pairs
 
-    @pl.loop(1, seq)
+    @pl.loop(1, seq, unroll=31)
     def _(r):
         pl.semaphore_signal(barrier, inc=1, device_id=(group, lax.rem(me + r, seq)), device_id_type=MESH)
 
-    @pl.loop(1, dps)
+    @pl.loop(1, dps, unroll=7)
     def _(r):
         for side in range(2):
             pl.semaphore_signal(

time: 165 us -> 164 us (level)
  no operation moved by 1% of the time
where the time goes in v5:
time: 164 us
  Pallas kernels  164 us (100%)
    pallas_call x1, Pallas kernels, step(): pl.pallas_call(functools.partial(kernel, pairs, dps, 1.0 / math.sqrt(samp...  162 us

profile of v5, /device:TPU:32, one launch (start us, length us, event | category | flops | bytes accessed | tf_op | source)
XLA Modules:
  0.0 164.3 jit_solution(2429759936458593399)
XLA Ops:
  0.6 161.9 %shard_map.101 = (bf16[2,64,4096]{2,1,0:T(8,128)(2,1)S(1)}, bf16[2,64,4096]{2,1,0:T(8,128)(2,1)S(1)}, bf16[2,64,4096]{2,1,0:T(8,128)(2,1)S(1)}, f32[1,128]{1,0:T(1,128)S(1)}, f32[1,128]{1,0:T(1,128)S(1)}) custom-call(bf16[2,64,4096]{2,1,0:T(8,128)(2,1)} %q_in.1, bf16[2,64,4096]{2,1,0:T(8,128)(2,1)} %g_in.1, bf16[2,64,4096]{2,1,0:T(8,128)(2,1)} %k_in.1, ...), custom_call_target="tpu_custom_call" | custom-call | tf_op jit(solution)/shard_map/pallas_call | solution.py:415
  162.5 1.7 %shard_map.102 = (bf16[2,64,4096]{2,1,0:T(8,128)(2,1)}, bf16[2,64,4096]{2,1,0:T(8,128)(2,1)}, bf16[2,64,4096]{2,1,0:T(8,128)(2,1)}, f32[1,128]{1,0:T(1,128)}, f32[1,128]{1,0:T(1,128)}) custom-call(bf16[2,64,4096]{2,1,0:T(8,128)(2,1)S(1)} %get-tuple-element.10.refs_0_, bf16[2,64,4096]{2,1,0:T(8,128)(2,1)S(1)} %get-tuple-element.11.refs_1_, ...), custom_call_target="tpu_custom_call" | custom-call | tf_op jit(solution)/shard_map/pallas_call | solution.py:454
